TPU v7x, 32 devices: a whole 2x2x4 slice. The times are simulated.
32 devices in a mesh: seq: 16 (over z, y, core), head: 1, dp: 2 (over x).
Axes of the slice: x: 2, y: 2, z: 4, core: 2. Of those that a mesh axis runs over, the one named last changes fastest.
Arguments:
- queries: bfloat16 [22528, 2048], P(('dp', 'seq'), 'head'), parts along dimension 0, may hold values from -96 to 96
- out_grad: bfloat16 [22528, 2048], P(('dp', 'seq'), 'head'), parts along dimension 0, may hold values from -16 to 16
- encodings: bfloat16 [320, 16, 2048], P(('dp', 'seq'), None, 'head'), parts along dimension 0, may hold values from -6 to 6
- key_weight: bfloat16 [2048, 2048], P(None, 'head'), may hold values from -0.125 to 0.125
- value_weight: bfloat16 [2048, 2048], P(None, 'head'), may hold values from -0.125 to 0.125
- neighbours: int32 [352, 2], P(('dp', 'seq')), parts along dimension 0, may hold values from 0 to 159, as said below
Outputs:
- query_grad: bfloat16 [22528, 2048], P(('dp', 'seq'), 'head'), parts along dimension 0
- encoding_grad: bfloat16 [320, 16, 2048], P(('dp', 'seq'), None, 'head'), parts along dimension 0
There are 2 independent parts, one for each index of `dp`. A program takes and returns all parts, laid end to end along the dimension named above; an argument that names none is the same for every part. Nothing has to cross between parts.
Inputs may be any that keep to these rules, and one draw needn't show every extreme that they name: `neighbours`: row r of encodings is held by index r // 10 of seq. In each aligned block of 11 spans, at most 2 of the 22 ids belong to one holder, and some holder has exactly 2. A span's two ids differ.
All inputs are finite; a program needn't handle non-finite values.
Results may differ from a plain program's by a relative error of at most 0.011.
Values may be sent and summed in bfloat16 or wider, within the bound.
A program may use at most 64 MiB of HBM per device.

v0:
```python
import math

import jax
import jax.numpy as jnp
from jax import lax
from jax.sharding import PartitionSpec as P

D = 2048
HEADS = 16


def slot_ranks(owner_ids):
    count = owner_ids.shape[-1]
    same_owner = owner_ids[..., :, None] == owner_ids[..., None, :]
    positions = jnp.arange(count, dtype=jnp.int32)
    earlier = positions[None, :] < positions[:, None]
    return jnp.sum(same_owner & earlier, axis=-1)


def on_device(queries, out_grad, encodings, key_weight, value_weight, neighbours):
    seq_count = lax.axis_size("seq")
    seq_index = lax.axis_index("seq")
    spans_here = neighbours.shape[0]
    ref_count = 2 * spans_here
    rows_here, neighbour_len, half_width = encodings.shape
    full_width = key_weight.shape[0]
    tok_rows = queries.shape[0]
    span_len = tok_rows // spans_here
    head_size = D // HEADS
    heads_here = half_width // head_size
    scaling = 1.0 / math.sqrt(head_size)
    capacity = max(2, ref_count // seq_count)
    slot_count = seq_count * capacity
    all_lists = lax.all_gather(neighbours, "seq", axis=0, tiled=True).reshape(seq_count, ref_count)
    owner_table = all_lists // rows_here
    local_table = all_lists % rows_here
    rank_table = slot_ranks(owner_table)
    own_ids = neighbours.reshape(ref_count)
    own_owner = own_ids // rows_here
    position = own_owner * capacity + slot_ranks(own_owner)
    slot_ids = jnp.arange(capacity, dtype=jnp.int32)
    chosen = (owner_table == seq_index)[:, None, :] & (
        rank_table[:, None, :] == slot_ids[None, :, None]
    )
    filled = jnp.any(chosen, axis=-1)
    slot_row = jnp.sum(jnp.where(chosen, local_table[:, None, :], 0), axis=-1)
    select = filled[..., None] & (
        slot_row[..., None] == jnp.arange(rows_here, dtype=jnp.int32)[None, None, :]
    )
    select = select.astype(jnp.bfloat16).reshape(slot_count, rows_here)
    flat_enc = encodings.reshape(rows_here, neighbour_len * half_width)
    outgoing = jnp.dot(select, flat_enc, preferred_element_type=jnp.float32).astype(jnp.bfloat16)
    outgoing = outgoing.reshape(seq_count, capacity, neighbour_len, half_width)
    arrived = lax.all_to_all(outgoing, "seq", split_axis=0, concat_axis=0, tiled=True)
    flat_arrived = arrived.reshape(slot_count, neighbour_len, half_width)
    whole = lax.all_gather(flat_arrived, "head", axis=2, tiled=True)
    full_rows = jnp.take(whole, position, axis=0)
    flat_rows = full_rows.reshape(ref_count * neighbour_len, full_width)
    keys = jnp.dot(flat_rows, key_weight, preferred_element_type=jnp.float32).astype(jnp.bfloat16)
    values = jnp.dot(flat_rows, value_weight, preferred_element_type=jnp.float32).astype(
        jnp.bfloat16
    )
    query_heads = queries.reshape(spans_here, span_len, heads_here, head_size)
    grad_heads = out_grad.reshape(spans_here, span_len, heads_here, head_size)
    key_heads = keys.reshape(spans_here, 2 * neighbour_len, heads_here, head_size)
    value_heads = values.reshape(spans_here, 2 * neighbour_len, heads_here, head_size)
    scores = (
        jnp.einsum("cthd,cuhd->chtu", query_heads, key_heads, preferred_element_type=jnp.float32)
        * scaling
    )
    scores = scores - jnp.max(scores, axis=-1, keepdims=True)
    raised = jnp.exp(scores)
    probs = raised / jnp.sum(raised, axis=-1, keepdims=True)
    probs_b = probs.astype(jnp.bfloat16)
    attended = jnp.einsum(
        "chtu,cuhd->cthd", probs_b, value_heads, preferred_element_type=jnp.float32
    )
    delta = jnp.transpose(jnp.sum(grad_heads.astype(jnp.float32) * attended, axis=-1), (0, 2, 1))
    dprobs = jnp.einsum(
        "cthd,cuhd->chtu", grad_heads, value_heads, preferred_element_type=jnp.float32
    )
    dscores = (probs * (dprobs - delta[..., None])).astype(jnp.bfloat16)
    query_grad = (
        jnp.einsum("chtu,cuhd->cthd", dscores, key_heads, preferred_element_type=jnp.float32)
        * scaling
    )
    query_grad = query_grad.astype(jnp.bfloat16).reshape(tok_rows, half_width)
    key_grad = (
        jnp.einsum("chtu,cthd->cuhd", dscores, query_heads, preferred_element_type=jnp.float32)
        * scaling
    )
    key_grad = key_grad.astype(jnp.bfloat16).reshape(ref_count * neighbour_len, half_width)
    value_grad = jnp.einsum(
        "chtu,cthd->cuhd", probs_b, grad_heads, preferred_element_type=jnp.float32
    )
    value_grad = value_grad.astype(jnp.bfloat16).reshape(ref_count * neighbour_len, half_width)
    contract = (((1,), (1,)), ((), ()))
    partial_value = lax.dot_general(
        key_grad, key_weight, contract, preferred_element_type=jnp.float32
    )
    partial_value = partial_value + lax.dot_general(
        value_grad, value_weight, contract, preferred_element_type=jnp.float32
    )
    summed = lax.psum_scatter(
        partial_value.reshape(ref_count, neighbour_len, full_width),
        "head",
        scatter_dimension=2,
        tiled=True,
    )
    ref_grad = summed.astype(jnp.bfloat16)
    returning = (
        jnp.zeros((slot_count, neighbour_len, half_width), jnp.bfloat16).at[position].set(ref_grad)
    )
    returning = returning.reshape(seq_count, capacity, neighbour_len, half_width)
    came_back = lax.all_to_all(returning, "seq", split_axis=0, concat_axis=0, tiled=True).reshape(
        slot_count, neighbour_len * half_width
    )
    encoding_grad = lax.dot_general(
        select, came_back, (((0,), (0,)), ((), ())), preferred_element_type=jnp.float32
    )
    encoding_grad = encoding_grad.astype(jnp.bfloat16).reshape(rows_here, neighbour_len, half_width)
    return (query_grad, encoding_grad)


def solution(mesh):
    return jax.shard_map(
        on_device,
        mesh=mesh,
        in_specs=(
            P(("dp", "seq"), "head"),
            P(("dp", "seq"), "head"),
            P(("dp", "seq"), None, "head"),
            P(None, "head"),
            P(None, "head"),
            P(("dp", "seq"), None),
        ),
        out_specs=(P(("dp", "seq"), "head"), P(("dp", "seq"), None, "head")),
        check_vma=False,
    )
```

profile of v0, /device:TPU:15, one launch (start us, length us, event | category | flops | bytes accessed | tf_op | source)
XLA Modules:
  0.0 186.6 jit_solution(7928898060411556864)
XLA Ops:
  0.6 15.8 %all-gather = s32[16,11,2]{1,2,0:T(2,128)S(1)} all-gather(s32[1,11,2]{1,2,0:T(2,128)} %bitcast.118), channel_id=1, replica_groups=mesh['seq'=16,'head'=1,'dp'=2] {'seq'}, dimensions={0}, use_global_device_ids=true | all-gather | bytes 1496 | tf_op jit(solution)/shard_map/all_gather | solution.py:34
  16.5 0.1 copy.91
  16.6 0.1 copy.93
  16.7 0.1 copy.96
  16.8 0.1 copy.94
  17.0 0.1 copy.98
  17.0 0.5 convert_reduce_fusion
  17.6 0.1 copy.99
  17.7 0.1 fusion.44
  17.8 0.1 select_reduce_fusion
  17.9 0.1 copy.104
  18.0 0.1 eq.78
  18.1 0.1 copy.100
  18.2 0.1 and.96
  18.3 1.2 pad.1
  19.5 0.6 copy.119
  20.1 0.7 convolution_convert_fusion
  20.8 2.4 %copy.120 = bf16[4,8,16,2048]{3,2,1,0:T(8,128)(2,1)} copy(bf16[4,8,16,2048]{3,1,2,0:T(8,128)(2,1)S(1)} %bitcast.102) | data formatting | bytes 4194304
  23.3 11.1 %all-to-all-start = ((bf16[16,2,16,2048]{3,2,1,0:T(8,128)(2,1)}), bf16[16,2,16,2048]{3,2,1,0:T(8,128)(2,1)}, u32[]{:S(2)}, u32[]{:S(2)}) async-start(bf16[16,2,16,2048]{3,2,1,0:T(8,128)(2,1)} %bitcast.22), calls=%async_computation | async-start | bytes 4194304 | tf_op jit(solution)/shard_map/all_to_all | solution.py:54
  34.4 0.1 copy.90
  34.5 0.1 div.57
  34.6 0.1 div.60
  34.7 0.1 copy.89
  34.8 0.1 and.88
  34.9 0.1 and.100
  35.0 0.2 convert_reduce_fusion.1
  35.2 0.1 broadcast_in_dim.25
  35.3 0.1 broadcast_in_dim.26
  35.3 2.9 %copy.122 = bf16[88,8,16,128]{3,2,1,0:T(8,128)(2,1)S(1)} copy(bf16[88,8,16,128]{3,1,2,0:T(8,128)(2,1)} %bitcast.106) | data formatting | bytes 5767168
  38.2 2.5 %copy.124 = bf16[88,8,16,128]{3,2,1,0:T(8,128)(2,1)} copy(bf16[88,8,16,128]{3,1,2,0:T(8,128)(2,1)S(1)} %bitcast.107) | data formatting | bytes 5767168
  40.7 41.2 %all-to-all-done = bf16[16,2,16,2048]{3,2,1,0:T(8,128)(2,1)} async-done(((bf16[16,2,16,2048]{3,2,1,0:T(8,128)(2,1)}), bf16[16,2,16,2048]{3,2,1,0:T(8,128)(2,1)}, u32[]{:S(2)}, u32[]{:S(2)}) %all-to-all-start) | async-done | bytes 2097184 | tf_op jit(solution)/shard_map/all_to_all | solution.py:54
  81.9 3.4 %gather_fusion = bf16[22,16,2048]{2,1,0:T(8,128)(2,1)} fusion(bf16[32,16,2048]{2,1,0:T(8,128)(2,1)} %bitcast.1, s32[1024]{0:T(1024)S(1)} %pad_clamp_fusion), kind=kCustom, calls=%fused_computation | custom fusion | bytes 2883672 | tf_op jit(solution)/shard_map/jit(_take)/gather | solution.py:57
  85.3 1.6 bitcast_select_fusion
  86.9 6.5 %fusion.30 = bf16[44,8,16,128]{3,1,2,0:T(8,128)(2,1)S(1)} fusion(bf16[352,2048]{1,0:T(8,128)(2,1)S(1)} %bitcast_select_fusion, bf16[2048,2048]{1,0:T(8,128)(2,1)} %param.9), kind=kOutput, calls=%fused_computation.32 | convolution fusion | flops 2953510912 | bytes 11272192 | tf_op jit(solution)/shard_map/dot_general | solution.py:59
  93.4 0.4 copy.121
  93.8 1.6 fusion.8
  95.4 0.0 slice-start.2
  95.4 6.8 %fusion.58 = (f32[11,16,64]{2,1,0:T(8,128)S(1)}, f32[11,16,64,32]{2,3,1,0:T(8,128)S(1)}) fusion(f32[11,16,32,64]{3,2,1,0:T(8,128)S(1)} %fusion.8), kind=kOutput, calls=%fused_computation.79 | output fusion | flops 1441823 | bytes 2928640 | tf_op jit(solution)/shard_map/sub | solution.py:71
  102.2 0.0 slice-start.3
  102.2 0.9 fusion.27
  103.1 0.6 copy.118
  103.6 0.7 slice-done.3
  104.4 3.1 %fusion.31 = bf16[44,8,16,128]{3,1,2,0:T(8,128)(2,1)S(1)} fusion(bf16[352,2048]{1,0:T(8,128)(2,1)S(1)} %bitcast_select_fusion, bf16[2048,2048]{1,0:T(8,128)(2,1)S(1)} %bitcast.122), kind=kOutput, calls=%fused_computation.33 | convolution fusion | flops 2953510912 | bytes 11272192 | tf_op jit(solution)/shard_map/dot_general | solution.py:60
  107.5 0.4 copy.123
  107.9 0.0 slice-start
  107.9 2.6 %fusion.1 = f32[11,64,16]{1,2,0:T(8,128)S(1)} fusion(bf16[11,64,16,128]{3,2,1,0:T(8,128)(2,1)S(1)} %bitcast.109, bf16[11,32,16,128]{3,2,1,0:T(8,128)(2,1)S(1)} %bitcast.114, f32[11,16,64,32]{2,3,1,0:T(8,128)S(1)} %get-tuple-element.7, f32[11,16,64]{2,1,0:T(8,128)S(1)} %get-tuple-element.6), kind=kOutput, calls=%fused_computation.6 | convolution fusion | flops 97309696 | bytes 5857280 | tf_op jit(solution)/shard_map/chtu,cuhd->cthd/dot_general | solution.py:75
  110.5 0.0 slice-start.1
  110.5 1.6 fusion.3
  112.2 0.9 fusion.24
  113.0 0.2 copy-done.2
  113.3 0.6 copy.116
  113.9 3.4 %fusion.34 = f32[352,2048]{1,0:T(8,128)S(1)} fusion(bf16[2048,2048]{1,0:T(8,128)(2,1)S(1)} %bitcast.120, bf16[44,8,16,128]{3,2,1,0:T(8,128)(2,1)S(1)} %bitcast.117), kind=kOutput, calls=%fused_computation.36 | convolution fusion | flops 2952790016 | bytes 12713984 | tf_op jit(solution)/shard_map/dot_general | solution.py:98
  117.3 6.6 %add_convert_fusion = bf16[352,2048]{1,0:T(8,128)(2,1)S(1)} fusion(f32[352,2048]{1,0:T(8,128)S(1)} %fusion.34, bf16[2048,2048]{1,0:T(8,128)(2,1)} %param.10, bf16[44,8,16,128]{3,2,1,0:T(8,128)(2,1)S(1)} %bitcast.113), kind=kOutput, calls=%fused_computation.16 | convolution fusion | flops 2954231808 | bytes 14155776 | tf_op jit(solution)/shard_map/dot_general | solution.py:101
  123.8 1.6 broadcast_in_dim.34
  125.4 5.4 %scatter_fusion = bf16[32,16,2048]{2,1,0:T(8,128)(2,1)} fusion(bf16[32,16,2048]{2,1,0:T(8,128)(2,1)} %broadcast_in_dim.34, s32[22]{0:T(128)S(1)} %fusion.54, bf16[22,16,2048]{2,1,0:T(8,128)(2,1)S(1)} %bitcast.116), kind=kCustom, calls=%fused_computation.1 | custom fusion | bytes 4325464 | tf_op jit(solution)/shard_map/scatter | solution.py:112
  130.8 5.1 %all-to-all-start.1 = ((bf16[16,2,16,2048]{3,2,1,0:T(8,128)(2,1)}), bf16[16,2,16,2048]{3,2,1,0:T(8,128)(2,1)S(1)}, u32[]{:S(2)}, u32[]{:S(2)}) async-start(bf16[16,2,16,2048]{3,2,1,0:T(8,128)(2,1)} %bitcast.13), calls=%async_computation.1 | async-start | bytes 4194304 | tf_op jit(solution)/shard_map/all_to_all | solution.py:115
  136.0 2.6 %fusion.2 = bf16[11,64,16,128]{3,1,2,0:T(8,128)(2,1)S(1)} fusion(bf16[11,16,64,32]{2,3,1,0:T(8,128)(2,1)} %copy-done.2, bf16[11,32,16,128]{3,2,1,0:T(8,128)(2,1)S(1)} %bitcast.98), kind=kOutput, calls=%fused_computation.8 | convolution fusion | flops 95158272 | bytes 5046272 | tf_op jit(solution)/shard_map/chtu,cuhd->cthd/dot_general | solution.py:84
  138.6 2.2 %copy.114 = bf16[11,64,16,128]{3,2,1,0:T(8,128)(2,1)S(1)} copy(bf16[11,64,16,128]{3,1,2,0:T(8,128)(2,1)S(1)} %fusion.2) | data formatting | bytes 5767168 | tf_op jit(solution)/shard_map/convert_element_type | solution.py:87
  140.7 2.4 %copy.166 = bf16[88,8,16,128]{3,1,2,0:T(8,128)(2,1)} copy(bf16[88,8,16,128]{3,2,1,0:T(8,128)(2,1)S(1)} %bitcast.99) | data formatting | bytes 5767168
  143.2 40.2 %all-to-all-done.1 = bf16[16,2,16,2048]{3,2,1,0:T(8,128)(2,1)S(1)} async-done(((bf16[16,2,16,2048]{3,2,1,0:T(8,128)(2,1)}), bf16[16,2,16,2048]{3,2,1,0:T(8,128)(2,1)S(1)}, u32[]{:S(2)}, u32[]{:S(2)}) %all-to-all-start.1) | async-done | bytes 2097184 | tf_op jit(solution)/shard_map/all_to_all | solution.py:115
  183.4 1.2 copy.128
  184.5 0.6 convolution_convert_fusion.1
  185.1 0.6 copy.129
  185.7 0.9 slice.2
  (30 shorter events, 0.2 us)
Async XLA Ops:
  23.3 11.1 %copy-start.5 = (s32[11,2]{0,1:T(2,128)S(1)}, s32[11,2]{0,1:T(2,128)}, u32[]{:S(2)}) copy-start(s32[11,2]{0,1:T(2,128)} %param.11) | copy-start | bytes 268
  23.3 58.6 %all-to-all-start = ((bf16[16,2,16,2048]{3,2,1,0:T(8,128)(2,1)}), bf16[16,2,16,2048]{3,2,1,0:T(8,128)(2,1)}, u32[]{:S(2)}, u32[]{:S(2)}) async-start(bf16[16,2,16,2048]{3,2,1,0:T(8,128)(2,1)} %bitcast.22), calls=%async_computation | async-start | bytes 4194304 | tf_op jit(solution)/shard_map/all_to_all | solution.py:54
  35.3 2.9 %copy-start.3 = (bf16[704,2048]{1,0:T(8,128)(2,1)S(1)}, bf16[704,2048]{1,0:T(8,128)(2,1)}, u32[]{:S(2)}) copy-start(bf16[704,2048]{1,0:T(8,128)(2,1)} %param.7) | copy-start | bytes 8650756
  93.8 1.6 copy-start
  95.4 6.8 %copy-start.4 = (bf16[88,8,16,128]{3,2,1,0:T(8,128)(2,1)S(1)}, bf16[88,8,16,128]{3,2,1,0:T(8,128)(2,1)}, u32[]{:S(2)}) copy-start(bf16[88,8,16,128]{3,2,1,0:T(8,128)(2,1)} %copy.124) | copy-start | bytes 8650756
  95.4 8.3 %slice-start.2 = ((s8[8388608]{0:T(1024)(128)(4,1)}), s8[4194304]{0:T(1024)(128)(4,1)S(1)}, s32[]{:S(2)}) async-start(s8[8388608]{0:T(1024)(128)(4,1)} %bitcast.121), calls=%async_computation.4 | async-start | bytes 8388608
  102.2 2.2 %slice-start.3 = ((s8[8388608]{0:T(1024)(128)(4,1)}), s8[4194304]{0:T(1024)(128)(4,1)S(1)}, s32[]{:S(2)}) async-start(s8[8388608]{0:T(1024)(128)(4,1)} %bitcast.121), calls=%async_computation.5 | async-start | bytes 8388608
  107.9 5.9 %slice-start = ((s8[8388608]{0:T(1024)(128)(4,1)}), s8[4194304]{0:T(1024)(128)(4,1)S(1)}, s32[]{:S(2)}) async-start(s8[8388608]{0:T(1024)(128)(4,1)} %bitcast.119), calls=%async_computation.2 | async-start | bytes 8388608
  110.5 3.3 %slice-start.1 = ((s8[8388608]{0:T(1024)(128)(4,1)}), s8[4194304]{0:T(1024)(128)(4,1)S(1)}, s32[]{:S(2)}) async-start(s8[8388608]{0:T(1024)(128)(4,1)} %bitcast.119), calls=%async_computation.3 | async-start | bytes 8388608
  112.1 1.1 copy-start.2
  130.8 5.1 %copy-start.1 = (bf16[44,8,16,128]{3,2,1,0:T(8,128)(2,1)S(1)}, bf16[44,8,16,128]{3,2,1,0:T(8,128)(2,1)}, u32[]{:S(2)}) copy-start(bf16[44,8,16,128]{3,2,1,0:T(8,128)(2,1)} %copy-done) | copy-start | bytes 4325380
  130.8 52.6 %all-to-all-start.1 = ((bf16[16,2,16,2048]{3,2,1,0:T(8,128)(2,1)}), bf16[16,2,16,2048]{3,2,1,0:T(8,128)(2,1)S(1)}, u32[]{:S(2)}, u32[]{:S(2)}) async-start(bf16[16,2,16,2048]{3,2,1,0:T(8,128)(2,1)} %bitcast.13), calls=%async_computation.1 | async-start | bytes 4194304 | tf_op jit(solution)/shard_map/all_to_all | solution.py:115
where the time goes:
time: 187 us
  waiting for transfers between devices  81.4 us (44%)
  local copies, waits for them, and re-layouts  31.7 us (17%)
  matrix products  31.1 us (17%)
  starting transfers between devices  16.2 us (9%)
  blocking collectives  15.8 us (8%)
  other arithmetic  9.37 us (5%)
    all_to_all x1, waiting for transfers between devices, on_device(): lax.all_to_all(outgoing, 'seq', split_axis=0, concat_axis=0, tiled=True)  41.2 us
    all_to_all x1, waiting for transfers between devices, on_device(): lax.all_to_all(returning, 'seq', split_axis=0, concat_axis=0, tiled=True)  40.2 us
    all_gather x1, blocking collectives, on_device(): lax.all_gather(neighbours, 'seq', axis=0, tiled=True)  15.8 us
    unnamed x30, local copies, waits for them, and re-layouts  15.4 us
    all_to_all x1, starting transfers between devices, on_device(): lax.all_to_all(outgoing, 'seq', split_axis=0, concat_axis=0, tiled=True)  11.1 us
    sub x1, other arithmetic, on_device(): scores = scores - jnp.max(scores, axis=-1, keepdims=True)  6.75 us
    dot_general x1, matrix products, on_device(): lax.dot_general(value_grad, value_weight, contract, preferred_element_typ...  6.55 us
    dot_general x1, matrix products, on_device(): jnp.dot(flat_rows, key_weight, preferred_element_type=jnp.float32)  6.52 us
  transfers between devices with their start and end apart: 2, of which 2 were waited for; matrix products, arithmetic and copies ran while one was open for 7% of the time, Pallas kernels for 0%

commit v1 on v0

--- a/solution.py
+++ b/solution.py
@@ -1,12 +1,314 @@
+import functools
 import math
 
 import jax
 import jax.numpy as jnp
 from jax import lax
+from jax.experimental import pallas as pl
+from jax.experimental.pallas import tpu as pltpu
 from jax.sharding import PartitionSpec as P
 
 D = 2048
 HEADS = 16
+MESH = pl.DeviceIdType.MESH
+NT = (((1,), (1,)), ((), ()))
+TN = (((0,), (0,)), ((), ()))
+F32 = jnp.float32
+BF16 = jnp.bfloat16
+
+
+def one_hot(index, shape, dim):
+    places = lax.broadcasted_iota(jnp.int32, shape, dim)
+    return jnp.where(places == index, 1.0, 0.0).astype(BF16)
+
+
+def tile(j, size):
+    return pl.ds(pl.multiple_of(j * size, size), size)
+
+
+def greet(n, me):
+    barrier = pltpu.get_barrier_semaphore()
+
+    def signal(k, carry):
+        pl.semaphore_signal(
+            barrier, inc=1, device_id={"seq": lax.rem(me + k, n)}, device_id_type=MESH
+        )
+        return carry
+
+    lax.fori_loop(1, n, signal, 0)
+    pl.semaphore_wait(barrier, n - 1)
+
+
+def exchange(n, me, size, src, dst, send_sem, recv_sem, own_sem):
+    own = pltpu.make_async_copy(src.at[tile(me, size)], dst.at[tile(me, size)], own_sem)
+
+    def remote(k):
+        peer = lax.rem(me + k, n)
+        return pltpu.make_async_remote_copy(
+            src_ref=src.at[tile(peer, size)],
+            dst_ref=dst.at[tile(me, size)],
+            send_sem=send_sem.at[k],
+            recv_sem=recv_sem.at[k],
+            device_id={"seq": peer},
+            device_id_type=MESH,
+        )
+
+    def arrival(k):
+        holder = lax.rem(me + n - k, n)
+        return pltpu.make_async_remote_copy(
+            src_ref=src.at[tile(holder, size)],
+            dst_ref=dst.at[tile(holder, size)],
+            send_sem=send_sem.at[k],
+            recv_sem=recv_sem.at[k],
+            device_id={"seq": holder},
+            device_id_type=MESH,
+        )
+
+    def start(i, carry):
+        k = lax.rem(i + n // 2 - 1, n - 1) + 1
+        remote(k).start()
+        return carry
+
+    def finish(k, carry):
+        arrival(k).wait_recv()
+        remote(k).wait_send()
+        return carry
+
+    def start_all():
+        own.start()
+        lax.fori_loop(0, n - 1, start, 0)
+
+    def wait_all():
+        own.wait()
+        lax.fori_loop(1, n, finish, 0)
+
+    return start_all, wait_all
+
+
+def fetch_kernel(n, want_ref, enc_ref, arrived_ref, asked_out, asked, outgoing, s1, r1, s2, r2, own):
+    me = lax.axis_index("seq")
+    size = want_ref.shape[0] // n
+    greet(n, me)
+    start, wait = exchange(n, me, size, want_ref, asked, s1, r1, own.at[0])
+    start()
+    wait()
+    target = asked[:, 0:1]
+    asked_out[...] = asked[...]
+    select = one_hot(target, (asked.shape[0], enc_ref.shape[0]), 1)
+    width = 512
+
+    def column(j, carry):
+        cols = tile(j, width)
+        outgoing[:, cols] = jnp.dot(
+            select, enc_ref[:, cols], preferred_element_type=F32
+        ).astype(BF16)
+        return carry
+
+    lax.fori_loop(0, enc_ref.shape[1] // width, column, 0)
+    start, wait = exchange(n, me, size, outgoing, arrived_ref, s2, r2, own.at[1])
+    start()
+    wait()
+
+
+def give_back_kernel(n, asked_ref, returning_ref, grad_ref, came, s1, r1, own):
+    me = lax.axis_index("seq")
+    size = asked_ref.shape[0] // n
+    greet(n, me)
+    start, wait = exchange(n, me, size, returning_ref, came, s1, r1, own.at[0])
+    start()
+    select = one_hot(asked_ref[:, 0:1], (asked_ref.shape[0], grad_ref.shape[0]), 1)
+    wait()
+    width = 512
+
+    def column(j, carry):
+        cols = tile(j, width)
+        grad_ref[:, cols] = lax.dot_general(
+            select, came[:, cols], TN, preferred_element_type=F32
+        ).astype(BF16)
+        return carry
+
+    lax.fori_loop(0, grad_ref.shape[1] // width, column, 0)
+
+
+def reader_kernel(
+    spans, place_ref, place_row, arr_hbm, q_hbm, g_hbm, wk_hbm, wv_hbm, qg_hbm, ret_hbm,
+    arr, q, g, wk, wv, qg, picked, keys, vals, kg, vg, ret, sem, wsem, osem,
+):
+    width = 256
+    parts = 4
+    wide = wk.shape[1] // parts
+    head = D // HEADS
+    span = q.shape[0] // spans
+    pair = keys.shape[0] // spans
+    scaling = 1.0 / math.sqrt(head)
+    first = pltpu.make_async_copy(arr_hbm, arr, sem.at[0])
+    first.start()
+    weights = []
+    for j in range(parts):
+        cols = pl.ds(j * wide, wide)
+        both = [
+            pltpu.make_async_copy(h.at[:, cols], v.at[:, cols], wsem.at[i, j])
+            for i, (h, v) in enumerate(((wk_hbm, wk), (wv_hbm, wv)))
+        ]
+        for copy in both:
+            copy.start()
+        weights.append(both)
+    loads = [
+        pltpu.make_async_copy(q_hbm, q, sem.at[1]),
+        pltpu.make_async_copy(g_hbm, g, sem.at[2]),
+    ]
+    for copy in loads:
+        copy.start()
+    count, slots = keys.shape[0], arr.shape[0]
+    first.wait()
+    gather = one_hot(place_ref[:, 0:1], (count, slots), 1)
+
+    def pick(j, carry):
+        cols = tile(j, width)
+        picked[:, cols] = jnp.dot(gather, arr[:, cols], preferred_element_type=F32).astype(BF16)
+        return carry
+
+    lax.fori_loop(0, D // width, pick, 0)
+
+    def project(j, carry):
+        cols = tile(j, width)
+        keys[:, cols] = jnp.dot(picked[...], wk[:, cols], preferred_element_type=F32).astype(BF16)
+        vals[:, cols] = jnp.dot(picked[...], wv[:, cols], preferred_element_type=F32).astype(BF16)
+        return carry
+
+    for j in range(parts):
+        for copy in weights[j]:
+            copy.wait()
+        lax.fori_loop(j * wide // width, (j + 1) * wide // width, project, 0)
+    for copy in loads:
+        copy.wait()
+
+    def attend(c, carry):
+        toks, nbrs = tile(c, span), tile(c, pair)
+        for h in range(HEADS):
+            cols = slice(h * head, (h + 1) * head)
+            qh, gh = q[toks, cols], g[toks, cols]
+            kh, vh = keys[nbrs, cols], vals[nbrs, cols]
+            scores = lax.dot_general(kh, qh, NT, preferred_element_type=F32) * scaling
+            raised = jnp.exp(scores - jnp.max(scores, axis=0, keepdims=True))
+            probs = raised / jnp.sum(raised, axis=0, keepdims=True)
+            probs_b = probs.astype(BF16)
+            dprobs = lax.dot_general(vh, gh, NT, preferred_element_type=F32)
+            delta = jnp.sum(probs_b.astype(F32) * dprobs, axis=0, keepdims=True)
+            dscores = (probs * (dprobs - delta)).astype(BF16)
+            dq = lax.dot_general(dscores, kh, TN, preferred_element_type=F32) * scaling
+            qg[toks, cols] = dq.astype(BF16)
+            dk = jnp.dot(dscores, qh, preferred_element_type=F32) * scaling
+            kg[nbrs, cols] = dk.astype(BF16)
+            vg[nbrs, cols] = jnp.dot(probs_b, gh, preferred_element_type=F32).astype(BF16)
+        pltpu.make_async_copy(qg.at[toks], qg_hbm.at[toks], osem.at[c]).start()
+        return carry
+
+    lax.fori_loop(0, spans, attend, 0)
+    spread = one_hot(place_row[0:1, :], (slots, count), 0)
+
+    def back(j, carry):
+        cols = tile(j, width)
+        total = lax.dot_general(kg[...], wk[cols, :], NT, preferred_element_type=F32)
+        total = total + lax.dot_general(vg[...], wv[cols, :], NT, preferred_element_type=F32)
+        ret[:, cols] = jnp.dot(
+            spread, total.astype(BF16), preferred_element_type=F32
+        ).astype(BF16)
+        return carry
+
+    lax.fori_loop(0, D // width, back, 0)
+    done = pltpu.make_async_copy(ret, ret_hbm, sem.at[3])
+    done.start()
+
+    def landed(c, carry):
+        toks = tile(c, span)
+        pltpu.make_async_copy(qg.at[toks], qg_hbm.at[toks], osem.at[c]).wait()
+        return carry
+
+    lax.fori_loop(0, spans, landed, 0)
+    done.wait()
+
+
+def on_device_whole_heads(queries, out_grad, encodings, key_weight, value_weight, neighbours):
+    n = lax.axis_size("seq")
+    spans = neighbours.shape[0]
+    refs = 2 * spans
+    rows, length, width = encodings.shape
+    toks = queries.shape[0]
+    capacity = max(2, refs // n)
+    slots = n * capacity
+    ids = neighbours.reshape(refs)
+    owner = ids // rows
+    place = owner * capacity + slot_ranks(owner)
+    hit = place[None, :] == jnp.arange(slots, dtype=jnp.int32)[:, None]
+    row = jnp.max(jnp.where(hit, (ids % rows)[None, :], -1), axis=1)
+    token = jnp.arange(length, dtype=jnp.int32)
+    want = jnp.where(row[:, None] >= 0, row[:, None] * length + token[None, :], -1)
+    want = jnp.broadcast_to(want.reshape(slots * length, 1), (slots * length, 128))
+    place = (place[:, None] * length + token[None, :]).reshape(refs * length)
+    place_col = jnp.broadcast_to(place[:, None], (refs * length, 128))
+    place_row = jnp.broadcast_to(place[None, :], (8, refs * length))
+    vmem = pl.BlockSpec(memory_space=pltpu.VMEM)
+    hbm = pl.BlockSpec(memory_space=pl.ANY)
+    dma = pltpu.SemaphoreType.DMA
+    total = slots * length
+    arrived, asked = pl.pallas_call(
+        functools.partial(fetch_kernel, n),
+        out_shape=(
+            jax.ShapeDtypeStruct((total, width), BF16),
+            jax.ShapeDtypeStruct((total, 128), jnp.int32),
+        ),
+        in_specs=[vmem, vmem],
+        out_specs=(hbm, vmem),
+        scratch_shapes=[
+            pltpu.VMEM((total, 128), jnp.int32),
+            pltpu.VMEM((total, width), BF16),
+            dma((n,)), dma((n,)), dma((n,)), dma((n,)), dma((2,)),
+        ],
+        compiler_params=pltpu.CompilerParams(
+            collective_id=0, has_side_effects=True, vmem_limit_bytes=16 << 20
+        ),
+    )(want, encodings.reshape(rows * length, width))
+    count = refs * length
+    query_grad, returning = pl.pallas_call(
+        functools.partial(reader_kernel, spans),
+        out_shape=(
+            jax.ShapeDtypeStruct((toks, width), BF16),
+            jax.ShapeDtypeStruct((total, width), BF16),
+        ),
+        in_specs=[vmem, vmem, hbm, hbm, hbm, hbm, hbm],
+        out_specs=(hbm, hbm),
+        scratch_shapes=[
+            pltpu.VMEM((total, width), BF16),
+            pltpu.VMEM((toks, width), BF16),
+            pltpu.VMEM((toks, width), BF16),
+            pltpu.VMEM((width, width), BF16),
+            pltpu.VMEM((width, width), BF16),
+            pltpu.VMEM((toks, width), BF16),
+            pltpu.VMEM((count, width), BF16),
+            pltpu.VMEM((count, width), BF16),
+            pltpu.VMEM((count, width), BF16),
+            pltpu.VMEM((count, width), BF16),
+            pltpu.VMEM((count, width), BF16),
+            pltpu.VMEM((total, width), BF16),
+            dma((4,)), dma((2, 4)), dma((spans,)),
+        ],
+        compiler_params=pltpu.CompilerParams(vmem_limit_bytes=56 << 20),
+    )(place_col, place_row, arrived, queries, out_grad, key_weight, value_weight)
+    encoding_grad = pl.pallas_call(
+        functools.partial(give_back_kernel, n),
+        out_shape=jax.ShapeDtypeStruct((rows * length, width), BF16),
+        in_specs=[vmem, hbm],
+        out_specs=vmem,
+        scratch_shapes=[
+            pltpu.VMEM((total, width), BF16),
+            dma((n,)), dma((n,)), dma((2,)),
+        ],
+        compiler_params=pltpu.CompilerParams(
+            collective_id=1, has_side_effects=True, vmem_limit_bytes=16 << 20
+        ),
+    )(asked, returning)
+    return query_grad, encoding_grad.reshape(rows, length, width)
 
 
 def slot_ranks(owner_ids):
@@ -54,7 +356,13 @@
     arrived = lax.all_to_all(outgoing, "seq", split_axis=0, concat_axis=0, tiled=True)
     flat_arrived = arrived.reshape(slot_count, neighbour_len, half_width)
     whole = lax.all_gather(flat_arrived, "head", axis=2, tiled=True)
-    full_rows = jnp.take(whole, position, axis=0)
+    pick = (position[:, None] == jnp.arange(slot_count, dtype=jnp.int32)[None, :]).astype(
+        jnp.bfloat16
+    )
+    full_rows = jnp.dot(
+        pick, whole.reshape(slot_count, neighbour_len * full_width),
+        preferred_element_type=jnp.float32,
+    ).astype(jnp.bfloat16)
     flat_rows = full_rows.reshape(ref_count * neighbour_len, full_width)
     keys = jnp.dot(flat_rows, key_weight, preferred_element_type=jnp.float32).astype(jnp.bfloat16)
     values = jnp.dot(flat_rows, value_weight, preferred_element_type=jnp.float32).astype(
@@ -123,8 +431,9 @@
 
 
 def solution(mesh):
+    body = on_device_whole_heads if mesh.shape["head"] == 1 else on_device
     return jax.shard_map(
-        on_device,
+        body,
         mesh=mesh,
         in_specs=(
             P(("dp", "seq"), "head"),

time: 187 us -> 191 us (1.021)
  Pallas kernels: 0 us -> 179 us
  waiting for transfers between devices: 81.4 us -> 0 us
  matrix products: 31.1 us -> 0 us
  local copies, waits for them, and re-layouts: 31.7 us -> 7.08 us
  starting transfers between devices: 16.2 us -> 0 us
  blocking collectives: 15.8 us -> 0 us
  other arithmetic: 9.37 us -> 1.82 us
    pallas_call x0 -> x3, Pallas kernels: none -> 179 us  [the longest x1 68.1 us: on_device_whole_heads(): pl.pallas_call(functools.partial(reader_kernel, spans), out_shape=(jax.Sh...]
    all_to_all x2 -> x0, waiting for transfers between devices: 81.4 us -> none  [the longest x1 41.2 us: on_device(): lax.all_to_all(outgoing, 'seq', split_axis=0, concat_axis=0, tiled=True)]
    dot_general x12 -> x0, matrix products: 31.1 us -> none  [the longest x1 6.55 us: on_device(): lax.dot_general(value_grad, value_weight, contract, preferred_element_typ...]
    all_to_all x2 -> x0, starting transfers between devices: 16.2 us -> none  [the longest x1 11.1 us: on_device(): lax.all_to_all(outgoing, 'seq', split_axis=0, concat_axis=0, tiled=True)]
    all_gather x1 -> x0, blocking collectives: 15.8 us -> none  [on_device(): lax.all_gather(neighbours, 'seq', axis=0, tiled=True)]
    unnamed x30 -> x7, local copies, waits for them, and re-layouts: 15.4 us -> 4.84 us
    sub x1 -> x0, other arithmetic: 6.75 us -> none  [on_device(): scores = scores - jnp.max(scores, axis=-1, keepdims=True)]
    scatter x1 -> x0, local copies, waits for them, and re-layouts: 5.41 us -> none  [on_device(): jnp.zeros((slot_count, neighbour_len, half_width), jnp.bfloat16)]
  transfers between devices with their start and end apart: 2 -> 0, of which waited for: 2 -> 0; matrix products, arithmetic and copies ran while one was open for 7% -> 0% of each run, Pallas kernels for 0% -> 0%
where the time goes in v1:
time: 191 us; the launch traced here: 189 us
  Pallas kernels  179 us (94%)
  local copies, waits for them, and re-layouts  7.08 us (4%)
    pallas_call x1, Pallas kernels, on_device_whole_heads(): pl.pallas_call(functools.partial(reader_kernel, spans), out_shape=(jax.Sh...  68.1 us
    pallas_call x1, Pallas kernels, on_device_whole_heads(): pl.pallas_call(functools.partial(fetch_kernel, n), out_shape=(jax.ShapeDt...  59.6 us
    pallas_call x1, Pallas kernels, on_device_whole_heads(): pl.pallas_call(functools.partial(give_back_kernel, n), out_shape=jax.Shap...  51.5 us
    unnamed x7, local copies, waits for them, and re-layouts  4.84 us

profile of v1, /device:TPU:15, one launch (start us, length us, event | category | flops | bytes accessed | tf_op | source)
XLA Modules:
  0.0 188.9 jit_solution(6989710906894209614)
XLA Ops:
  0.6 0.7 sign_compare_fusion
  1.3 0.1 copy.14
  1.4 0.1 ne.58
  1.5 0.7 broadcast_remainder_fusion
  2.2 0.1 copy.15
  2.3 0.1 rem.36
  2.4 0.1 copy.16
  2.5 0.1 div.24
  2.6 0.2 convert_reduce_fusion
  2.8 0.1 select_reduce_fusion
  2.9 0.1 iota_add_fusion
  3.0 0.1 add.82
  3.1 0.6 broadcast_in_dim.31.place_row
  3.7 0.1 add_select_fusion
  3.7 0.1 select_n.49
  3.8 0.8 broadcast_in_dim.30.place_ref
  4.6 0.1 broadcast_in_dim.36.want_ref
  4.7 0.0 copy-start.2
  4.7 1.1 copy-done.2
  5.8 59.6 %shard_map.77 = (bf16[512,2048]{1,0:T(8,128)(2,1)S(1)}, s32[512,128]{1,0:T(8,128)S(1)}) custom-call(s32[512,128]{1,0:T(8,128)S(1)} %broadcast_in_dim.36.want_ref, bf16[160,2048]{1,0:T(8,128)(2,1)S(1)} %bitcast.3), custom_call_target="tpu_custom_call" | custom-call | tf_op jit(solution)/shard_map/pallas_call | solution.py:255
  65.5 0.0 copy-start.1
  65.5 1.3 copy-done.1
  66.8 68.1 %shard_map.78 = (bf16[704,2048]{1,0:T(8,128)(2,1)}, bf16[512,2048]{1,0:T(8,128)(2,1)}) custom-call(s32[352,128]{1,0:T(8,128)} %broadcast_in_dim.30.place_ref, s32[8,352]{1,0:T(8,128)} %broadcast_in_dim.31.place_row, bf16[512,2048]{1,0:T(8,128)(2,1)} %copy-done.1, bf16[704,2048]{1,0:T(8,128)(2,1)} %q_hbm.1, bf16[704,2048]{1,0:T(8,128)(2,1)} %g_hbm.1, ...), custom_call_target="tpu_custom_call" | custom-call | tf_op jit(solution)/shard_map/pallas_call | solution.py:273
  134.9 0.0 copy-start
  134.9 1.6 copy-done
  136.5 51.5 %shard_map.79 = bf16[160,2048]{1,0:T(8,128)(2,1)S(1)} custom-call(s32[512,128]{1,0:T(8,128)S(1)} %get-tuple-element.8.asked_ref, bf16[512,2048]{1,0:T(8,128)(2,1)S(1)} %copy-done), custom_call_target="tpu_custom_call" | custom-call | tf_op jit(solution)/shard_map/pallas_call | solution.py:298
  188.1 0.8 copy.18
  (4 shorter events, 0.0 us)
Async XLA Ops:
  4.7 1.1 copy-start.2
  65.5 1.3 copy-start.1
  134.9 1.6 copy-start

commit v2 on v1

--- a/solution.py
+++ b/solution.py
@@ -39,14 +39,17 @@
     pl.semaphore_wait(barrier, n - 1)
 
 
-def exchange(n, me, size, src, dst, send_sem, recv_sem, own_sem):
-    own = pltpu.make_async_copy(src.at[tile(me, size)], dst.at[tile(me, size)], own_sem)
+def exchange(n, me, size, src, dst, cols, send_sem, recv_sem, own_sem):
+    def block(ref, p):
+        return ref.at[tile(p, size), cols]
+
+    own = pltpu.make_async_copy(block(src, me), block(dst, me), own_sem)
 
     def remote(k):
         peer = lax.rem(me + k, n)
         return pltpu.make_async_remote_copy(
-            src_ref=src.at[tile(peer, size)],
-            dst_ref=dst.at[tile(me, size)],
+            src_ref=block(src, peer),
+            dst_ref=block(dst, me),
             send_sem=send_sem.at[k],
             recv_sem=recv_sem.at[k],
             device_id={"seq": peer},
@@ -56,8 +59,8 @@
     def arrival(k):
         holder = lax.rem(me + n - k, n)
         return pltpu.make_async_remote_copy(
-            src_ref=src.at[tile(holder, size)],
-            dst_ref=dst.at[tile(holder, size)],
+            src_ref=block(src, holder),
+            dst_ref=block(dst, holder),
             send_sem=send_sem.at[k],
             recv_sem=recv_sem.at[k],
             device_id={"seq": holder},
@@ -65,12 +68,14 @@
         )
 
     def start(i, carry):
-        k = lax.rem(i + n // 2 - 1, n - 1) + 1
-        remote(k).start()
-        return carry
-
-    def finish(k, carry):
+        remote(lax.rem(i + n // 2 - 1, n - 1) + 1).start()
+        return carry
+
+    def received(k, carry):
         arrival(k).wait_recv()
+        return carry
+
+    def sent(k, carry):
         remote(k).wait_send()
         return carry
 
@@ -78,155 +83,174 @@
         own.start()
         lax.fori_loop(0, n - 1, start, 0)
 
-    def wait_all():
+    def wait_received():
         own.wait()
-        lax.fori_loop(1, n, finish, 0)
-
-    return start_all, wait_all
-
-
-def fetch_kernel(n, want_ref, enc_ref, arrived_ref, asked_out, asked, outgoing, s1, r1, s2, r2, own):
+        lax.fori_loop(1, n, received, 0)
+
+    def wait_sent():
+        lax.fori_loop(1, n, sent, 0)
+
+    return start_all, wait_received, wait_sent
+
+
+def kernel(
+    n, spans, want_ref, place_ref, place_row, enc_ref, q_hbm, g_hbm, wk_hbm, wv_hbm,
+    qg_hbm, grad_ref,
+    asked, outgoing, arr, q, g, wk, wv, qg, key_sum, val_sum, keys, vals, kg, vg, ret, came,
+    sem, wsem, own, ids_s, ids_r, out_s, out_r, back_s, back_r,
+):
     me = lax.axis_index("seq")
-    size = want_ref.shape[0] // n
-    greet(n, me)
-    start, wait = exchange(n, me, size, want_ref, asked, s1, r1, own.at[0])
-    start()
-    wait()
-    target = asked[:, 0:1]
-    asked_out[...] = asked[...]
-    select = one_hot(target, (asked.shape[0], enc_ref.shape[0]), 1)
-    width = 512
-
-    def column(j, carry):
-        cols = tile(j, width)
-        outgoing[:, cols] = jnp.dot(
-            select, enc_ref[:, cols], preferred_element_type=F32
-        ).astype(BF16)
-        return carry
-
-    lax.fori_loop(0, enc_ref.shape[1] // width, column, 0)
-    start, wait = exchange(n, me, size, outgoing, arrived_ref, s2, r2, own.at[1])
-    start()
-    wait()
-
-
-def give_back_kernel(n, asked_ref, returning_ref, grad_ref, came, s1, r1, own):
-    me = lax.axis_index("seq")
-    size = asked_ref.shape[0] // n
-    greet(n, me)
-    start, wait = exchange(n, me, size, returning_ref, came, s1, r1, own.at[0])
-    start()
-    select = one_hot(asked_ref[:, 0:1], (asked_ref.shape[0], grad_ref.shape[0]), 1)
-    wait()
-    width = 512
-
-    def column(j, carry):
-        cols = tile(j, width)
-        grad_ref[:, cols] = lax.dot_general(
-            select, came[:, cols], TN, preferred_element_type=F32
-        ).astype(BF16)
-        return carry
-
-    lax.fori_loop(0, grad_ref.shape[1] // width, column, 0)
-
-
-def reader_kernel(
-    spans, place_ref, place_row, arr_hbm, q_hbm, g_hbm, wk_hbm, wv_hbm, qg_hbm, ret_hbm,
-    arr, q, g, wk, wv, qg, picked, keys, vals, kg, vg, ret, sem, wsem, osem,
-):
+    parts = own.shape[1]
+    wide = enc_ref.shape[1] // parts
     width = 256
-    parts = 4
-    wide = wk.shape[1] // parts
     head = D // HEADS
     span = q.shape[0] // spans
     pair = keys.shape[0] // spans
+    size = want_ref.shape[0] // n
+    count, slots, held = keys.shape[0], arr.shape[0], enc_ref.shape[0]
     scaling = 1.0 / math.sqrt(head)
-    first = pltpu.make_async_copy(arr_hbm, arr, sem.at[0])
-    first.start()
+
     weights = []
     for j in range(parts):
-        cols = pl.ds(j * wide, wide)
+        rows = pl.ds(j * wide, wide)
         both = [
-            pltpu.make_async_copy(h.at[:, cols], v.at[:, cols], wsem.at[i, j])
+            pltpu.make_async_copy(h.at[rows], v.at[rows], wsem.at[i, j])
             for i, (h, v) in enumerate(((wk_hbm, wk), (wv_hbm, wv)))
         ]
         for copy in both:
             copy.start()
         weights.append(both)
     loads = [
-        pltpu.make_async_copy(q_hbm, q, sem.at[1]),
-        pltpu.make_async_copy(g_hbm, g, sem.at[2]),
+        pltpu.make_async_copy(q_hbm, q, sem.at[0]),
+        pltpu.make_async_copy(g_hbm, g, sem.at[1]),
     ]
     for copy in loads:
         copy.start()
-    count, slots = keys.shape[0], arr.shape[0]
-    first.wait()
+
+    greet(n, me)
+    start, received, sent = exchange(
+        n, me, size, want_ref, asked, slice(None), ids_s, ids_r, sem.at[2]
+    )
+    start()
+    received()
+    sent()
+    select = one_hot(asked[:, 0:1], (slots, held), 1)
+
+    def fetch(j):
+        return exchange(
+            n, me, size, outgoing, arr, tile(j, wide), out_s.at[j], out_r.at[j], own.at[0, j]
+        )
+
+    def serve(j, carry):
+        cols = tile(j, wide)
+        outgoing[:, cols] = jnp.dot(
+            select, enc_ref[:, cols], preferred_element_type=F32
+        ).astype(BF16)
+        fetch(j)[0]()
+        return carry
+
+    lax.fori_loop(0, parts, serve, 0)
+
     gather = one_hot(place_ref[:, 0:1], (count, slots), 1)
-
-    def pick(j, carry):
-        cols = tile(j, width)
-        picked[:, cols] = jnp.dot(gather, arr[:, cols], preferred_element_type=F32).astype(BF16)
-        return carry
-
-    lax.fori_loop(0, D // width, pick, 0)
-
-    def project(j, carry):
-        cols = tile(j, width)
-        keys[:, cols] = jnp.dot(picked[...], wk[:, cols], preferred_element_type=F32).astype(BF16)
-        vals[:, cols] = jnp.dot(picked[...], wv[:, cols], preferred_element_type=F32).astype(BF16)
-        return carry
-
     for j in range(parts):
         for copy in weights[j]:
             copy.wait()
-        lax.fori_loop(j * wide // width, (j + 1) * wide // width, project, 0)
+        fetch(j)[1]()
+        deep = slice(j * wide, (j + 1) * wide)
+        picked = jnp.dot(gather, arr[:, deep], preferred_element_type=F32).astype(BF16)
+
+        def project(i, carry):
+            cols = tile(i, width)
+            for w, total, result in ((wk, key_sum, keys), (wv, val_sum, vals)):
+                part = jnp.dot(picked, w[deep, cols], preferred_element_type=F32)
+                if j > 0:
+                    part = part + total[:, cols]
+                if j < parts - 1:
+                    total[:, cols] = part
+                else:
+                    result[:, cols] = part.astype(BF16)
+            return carry
+
+        lax.fori_loop(0, D // width, project, 0)
     for copy in loads:
         copy.wait()
 
-    def attend(c, carry):
-        toks, nbrs = tile(c, span), tile(c, pair)
-        for h in range(HEADS):
-            cols = slice(h * head, (h + 1) * head)
+    def attend(c, together):
+        toks = pl.ds(pl.multiple_of(c * span, span), together * span)
+        nbrs = pl.ds(pl.multiple_of(c * pair, pair), together * pair)
+        rows, lanes = 2 * together * pair, together * span
+        own = lax.rem(lax.broadcasted_iota(jnp.int32, (rows, lanes), 0) // pair, together)
+        mine = own == lax.broadcasted_iota(jnp.int32, (rows, lanes), 1) // span
+        gap = jnp.zeros((together * pair, head), BF16)
+
+        def apart(two):
+            upper = jnp.concatenate([two[:, :head], gap], axis=1)
+            return jnp.concatenate([upper, jnp.concatenate([gap, two[:, head:]], axis=1)], axis=0)
+
+        for h in range(0, HEADS, 2):
+            cols = slice(h * head, (h + 2) * head)
+            one, two = slice(h * head, (h + 1) * head), slice((h + 1) * head, (h + 2) * head)
+            half = together * pair
             qh, gh = q[toks, cols], g[toks, cols]
-            kh, vh = keys[nbrs, cols], vals[nbrs, cols]
+            kh, vh = apart(keys[nbrs, cols]), apart(vals[nbrs, cols])
             scores = lax.dot_general(kh, qh, NT, preferred_element_type=F32) * scaling
-            raised = jnp.exp(scores - jnp.max(scores, axis=0, keepdims=True))
-            probs = raised / jnp.sum(raised, axis=0, keepdims=True)
+            scores = jnp.where(mine, scores, -jnp.inf).reshape(2, half, lanes)
+            raised = jnp.exp(scores - jnp.max(scores, axis=1, keepdims=True))
+            probs = raised * (1.0 / jnp.sum(raised, axis=1, keepdims=True))
             probs_b = probs.astype(BF16)
             dprobs = lax.dot_general(vh, gh, NT, preferred_element_type=F32)
-            delta = jnp.sum(probs_b.astype(F32) * dprobs, axis=0, keepdims=True)
-            dscores = (probs * (dprobs - delta)).astype(BF16)
+            dprobs = dprobs.reshape(2, half, lanes)
+            delta = jnp.sum(probs_b.astype(F32) * dprobs, axis=1, keepdims=True)
+            dscores = (probs * (dprobs - delta)).astype(BF16).reshape(rows, lanes)
             dq = lax.dot_general(dscores, kh, TN, preferred_element_type=F32) * scaling
             qg[toks, cols] = dq.astype(BF16)
-            dk = jnp.dot(dscores, qh, preferred_element_type=F32) * scaling
-            kg[nbrs, cols] = dk.astype(BF16)
-            vg[nbrs, cols] = jnp.dot(probs_b, gh, preferred_element_type=F32).astype(BF16)
-        pltpu.make_async_copy(qg.at[toks], qg_hbm.at[toks], osem.at[c]).start()
-        return carry
-
-    lax.fori_loop(0, spans, attend, 0)
+            dk = jnp.dot(dscores, qh, preferred_element_type=F32)
+            kg[nbrs, one] = (dk[:half, :head] * scaling).astype(BF16)
+            kg[nbrs, two] = (dk[half:, head:] * scaling).astype(BF16)
+            dv = jnp.dot(probs_b.reshape(rows, lanes), gh, preferred_element_type=F32)
+            vg[nbrs, one] = dv[:half, :head].astype(BF16)
+            vg[nbrs, two] = dv[half:, head:].astype(BF16)
+
+    def attend_two(i, carry):
+        attend(i * 2, 2)
+        return carry
+
+    lax.fori_loop(0, spans // 2, attend_two, 0)
+    if spans % 2:
+        attend(spans - 1, 1)
+    query_done = pltpu.make_async_copy(qg, qg_hbm, sem.at[3])
+    query_done.start()
     spread = one_hot(place_row[0:1, :], (slots, count), 0)
 
+    def give_back(j):
+        return exchange(
+            n, me, size, ret, came, tile(j, wide), back_s.at[j], back_r.at[j], own.at[1, j]
+        )
+
     def back(j, carry):
-        cols = tile(j, width)
+        cols = tile(j, wide)
         total = lax.dot_general(kg[...], wk[cols, :], NT, preferred_element_type=F32)
         total = total + lax.dot_general(vg[...], wv[cols, :], NT, preferred_element_type=F32)
         ret[:, cols] = jnp.dot(
             spread, total.astype(BF16), preferred_element_type=F32
         ).astype(BF16)
-        return carry
-
-    lax.fori_loop(0, D // width, back, 0)
-    done = pltpu.make_async_copy(ret, ret_hbm, sem.at[3])
-    done.start()
-
-    def landed(c, carry):
-        toks = tile(c, span)
-        pltpu.make_async_copy(qg.at[toks], qg_hbm.at[toks], osem.at[c]).wait()
-        return carry
-
-    lax.fori_loop(0, spans, landed, 0)
-    done.wait()
+        give_back(j)[0]()
+        return carry
+
+    lax.fori_loop(0, parts, back, 0)
+
+    def finish(j, carry):
+        give_back(j)[1]()
+        cols = tile(j, wide)
+        grad_ref[:, cols] = lax.dot_general(
+            select, came[:, cols], TN, preferred_element_type=F32
+        ).astype(BF16)
+        fetch(j)[2]()
+        give_back(j)[2]()
+        return carry
+
+    lax.fori_loop(0, parts, finish, 0)
+    query_done.wait()
 
 
 def on_device_whole_heads(queries, out_grad, encodings, key_weight, value_weight, neighbours):
@@ -252,62 +276,44 @@
     hbm = pl.BlockSpec(memory_space=pl.ANY)
     dma = pltpu.SemaphoreType.DMA
     total = slots * length
-    arrived, asked = pl.pallas_call(
-        functools.partial(fetch_kernel, n),
+    count = refs * length
+    parts = 4
+    query_grad, encoding_grad = pl.pallas_call(
+        functools.partial(kernel, n, spans),
         out_shape=(
-            jax.ShapeDtypeStruct((total, width), BF16),
-            jax.ShapeDtypeStruct((total, 128), jnp.int32),
+            jax.ShapeDtypeStruct((toks, width), BF16),
+            jax.ShapeDtypeStruct((rows * length, width), BF16),
         ),
-        in_specs=[vmem, vmem],
+        in_specs=[vmem, vmem, vmem, vmem, hbm, hbm, hbm, hbm],
         out_specs=(hbm, vmem),
         scratch_shapes=[
             pltpu.VMEM((total, 128), jnp.int32),
             pltpu.VMEM((total, width), BF16),
-            dma((n,)), dma((n,)), dma((n,)), dma((n,)), dma((2,)),
-        ],
-        compiler_params=pltpu.CompilerParams(
-            collective_id=0, has_side_effects=True, vmem_limit_bytes=16 << 20
-        ),
-    )(want, encodings.reshape(rows * length, width))
-    count = refs * length
-    query_grad, returning = pl.pallas_call(
-        functools.partial(reader_kernel, spans),
-        out_shape=(
-            jax.ShapeDtypeStruct((toks, width), BF16),
-            jax.ShapeDtypeStruct((total, width), BF16),
-        ),
-        in_specs=[vmem, vmem, hbm, hbm, hbm, hbm, hbm],
-        out_specs=(hbm, hbm),
-        scratch_shapes=[
             pltpu.VMEM((total, width), BF16),
             pltpu.VMEM((toks, width), BF16),
             pltpu.VMEM((toks, width), BF16),
             pltpu.VMEM((width, width), BF16),
             pltpu.VMEM((width, width), BF16),
             pltpu.VMEM((toks, width), BF16),
-            pltpu.VMEM((count, width), BF16),
+            pltpu.VMEM((count, width), F32),
+            pltpu.VMEM((count, width), F32),
             pltpu.VMEM((count, width), BF16),
             pltpu.VMEM((count, width), BF16),
             pltpu.VMEM((count, width), BF16),
             pltpu.VMEM((count, width), BF16),
             pltpu.VMEM((total, width), BF16),
-            dma((4,)), dma((2, 4)), dma((spans,)),
-        ],
-        compiler_params=pltpu.CompilerParams(vmem_limit_bytes=56 << 20),
-    )(place_col, place_row, arrived, queries, out_grad, key_weight, value_weight)
-    encoding_grad = pl.pallas_call(
-        functools.partial(give_back_kernel, n),
-        out_shape=jax.ShapeDtypeStruct((rows * length, width), BF16),
-        in_specs=[vmem, hbm],
-        out_specs=vmem,
-        scratch_shapes=[
             pltpu.VMEM((total, width), BF16),
-            dma((n,)), dma((n,)), dma((2,)),
+            dma((4,)), dma((2, parts)), dma((2, parts)),
+            dma((n,)), dma((n,)),
+            dma((parts, n)), dma((parts, n)), dma((parts, n)), dma((parts, n)),
         ],
         compiler_params=pltpu.CompilerParams(
-            collective_id=1, has_side_effects=True, vmem_limit_bytes=16 << 20
+            collective_id=0, has_side_effects=True, vmem_limit_bytes=58 << 20
         ),
-    )(asked, returning)
+    )(
+        want, place_col, place_row, encodings.reshape(rows * length, width),
+        queries, out_grad, key_weight, value_weight,
+    )
     return query_grad, encoding_grad.reshape(rows, length, width)
 
 

time: 191 us -> 142 us (0.74)
  the two profiles are of different devices: /device:TPU:15 before, /device:TPU:0 now
where the time goes in v2:
time: 142 us
  Pallas kernels  131 us (92%)
  local copies, waits for them, and re-layouts  7.62 us (5%)
  other arithmetic  1.82 us (1%)
    pallas_call x1, Pallas kernels, on_device_whole_heads(): pl.pallas_call(functools.partial(kernel, n, spans), out_shape=(jax.ShapeD...  131 us
    unnamed x4, local copies, waits for them, and re-layouts  4.67 us

profile of v2, /device:TPU:0, one launch (start us, length us, event | category | flops | bytes accessed | tf_op | source)
XLA Modules:
  0.0 141.6 jit_solution(267322080960407503)
XLA Ops:
  0.6 0.7 sign_compare_fusion
  1.3 0.1 copy.14
  1.4 0.1 ne.58
  1.5 0.7 broadcast_divide_fusion
  2.2 0.1 copy.16
  2.3 0.1 div.24
  2.4 0.1 copy.15
  2.5 0.1 rem.36
  2.6 0.2 convert_reduce_fusion
  2.8 0.1 select_reduce_fusion
  2.9 0.1 iota_add_fusion
  3.0 0.1 add.86
  3.1 0.6 broadcast_in_dim.36.place_row
  3.7 0.1 add_select_fusion
  3.7 0.1 select_n.49
  3.8 0.8 broadcast_in_dim.35.place_ref
  4.6 0.8 broadcast_in_dim.34.want_ref
  5.4 131.5 %shard_map.77 = (bf16[704,2048]{1,0:T(8,128)(2,1)}, bf16[160,2048]{1,0:T(8,128)(2,1)}) custom-call(s32[512,128]{1,0:T(8,128)} %broadcast_in_dim.34.want_ref, s32[352,128]{1,0:T(8,128)} %broadcast_in_dim.35.place_ref, s32[8,352]{1,0:T(8,128)} %broadcast_in_dim.36.place_row, bf16[160,2048]{1,0:T(8,128)(2,1)} %bitcast.3, bf16[704,2048]{1,0:T(8,128)(2,1)} %q_hbm.1, ...), custom_call_target="tpu_custom_call" | custom-call | tf_op jit(solution)/shard_map/pallas_call | solution.py:281
  136.9 0.0 copy-start
  136.9 3.8 %copy.19 = bf16[704,2048]{1,0:T(8,128)(2,1)} copy(bf16[704,2048]{1,0:T(8,128)(2,1)} %get-tuple-element.14) | data formatting | bytes 5767168
  140.8 0.0 copy-done
  140.8 0.8 copy.20
  (4 shorter events, 0.0 us)
Async XLA Ops:
  136.9 3.8 %copy-start = (bf16[160,2048]{1,0:T(8,128)(2,1)S(1)}, bf16[160,2048]{1,0:T(8,128)(2,1)}, u32[]{:S(2)}) copy-start(bf16[160,2048]{1,0:T(8,128)(2,1)} %get-tuple-element.5) | copy-start | bytes 1966084

commit v3 on v2

--- a/solution.py
+++ b/solution.py
@@ -68,7 +68,7 @@
         )
 
     def start(i, carry):
-        remote(lax.rem(i + n // 2 - 1, n - 1) + 1).start()
+        remote(i + 1).start()
         return carry
 
     def received(k, carry):
@@ -94,9 +94,9 @@
 
 
 def kernel(
-    n, spans, want_ref, place_ref, place_row, enc_ref, q_hbm, g_hbm, wk_hbm, wv_hbm,
+    n, spans, length, plan_ref, enc_ref, q_hbm, g_hbm, wk_hbm, wv_hbm,
     qg_hbm, grad_ref,
-    asked, outgoing, arr, q, g, wk, wv, qg, key_sum, val_sum, keys, vals, kg, vg, ret, came,
+    want, asked, outgoing, arr, q, g, wk, wv, qg, key_sum, val_sum, keys, vals, kg, vg, ret, came,
     sem, wsem, own, ids_s, ids_r, out_s, out_r, back_s, back_r,
 ):
     me = lax.axis_index("seq")
@@ -106,7 +106,7 @@
     head = D // HEADS
     span = q.shape[0] // spans
     pair = keys.shape[0] // spans
-    size = want_ref.shape[0] // n
+    size = want.shape[0] // n
     count, slots, held = keys.shape[0], arr.shape[0], enc_ref.shape[0]
     scaling = 1.0 / math.sqrt(head)
 
@@ -127,9 +127,22 @@
     for copy in loads:
         copy.start()
 
+    def down(line, rows, each):
+        shape = (rows, line.shape[1])
+        here = lax.broadcasted_iota(jnp.int32, shape, 0) // each
+        here = here == lax.broadcasted_iota(jnp.int32, shape, 1)
+        picked_out = jnp.sum(jnp.where(here, line, 0.0), axis=1, keepdims=True)
+        return picked_out.astype(jnp.int32)
+
+    places = plan_ref[0:1, :].astype(F32)
+    token = lax.rem(lax.broadcasted_iota(jnp.int32, (slots, 1), 0), length)
+    row = down(plan_ref[1:2, :].astype(F32), slots, length)
+    row = jnp.where(row >= 0, row * length + token, -1)
+    want[...] = jnp.broadcast_to(row, want.shape)
+
     greet(n, me)
     start, received, sent = exchange(
-        n, me, size, want_ref, asked, slice(None), ids_s, ids_r, sem.at[2]
+        n, me, size, want, asked, slice(None), ids_s, ids_r, sem.at[2]
     )
     start()
     received()
@@ -151,7 +164,8 @@
 
     lax.fori_loop(0, parts, serve, 0)
 
-    gather = one_hot(place_ref[:, 0:1], (count, slots), 1)
+    place = down(places, count, length) * length + token[:count]
+    gather = one_hot(place, (count, slots), 1)
     for j in range(parts):
         for copy in weights[j]:
             copy.wait()
@@ -220,7 +234,13 @@
         attend(spans - 1, 1)
     query_done = pltpu.make_async_copy(qg, qg_hbm, sem.at[3])
     query_done.start()
-    spread = one_hot(place_row[0:1, :], (slots, count), 0)
+    refs = count // length
+    level = lax.broadcasted_iota(jnp.int32, (refs, count), 1)
+    here = lax.broadcasted_iota(jnp.int32, (refs, count), 0) == level // length
+    across = jnp.where(here, down(places, refs, 1), 0)
+    across = jnp.sum(across.astype(F32), axis=0, keepdims=True).astype(jnp.int32)
+    across = across * length + lax.rem(level[0:1, :], length)
+    spread = one_hot(across, (slots, count), 0)
 
     def give_back(j):
         return exchange(
@@ -266,12 +286,8 @@
     place = owner * capacity + slot_ranks(owner)
     hit = place[None, :] == jnp.arange(slots, dtype=jnp.int32)[:, None]
     row = jnp.max(jnp.where(hit, (ids % rows)[None, :], -1), axis=1)
-    token = jnp.arange(length, dtype=jnp.int32)
-    want = jnp.where(row[:, None] >= 0, row[:, None] * length + token[None, :], -1)
-    want = jnp.broadcast_to(want.reshape(slots * length, 1), (slots * length, 128))
-    place = (place[:, None] * length + token[None, :]).reshape(refs * length)
-    place_col = jnp.broadcast_to(place[:, None], (refs * length, 128))
-    place_row = jnp.broadcast_to(place[None, :], (8, refs * length))
+    lanes = -(-max(slots, refs) // 128) * 128
+    plan = jnp.stack([jnp.pad(place, (0, lanes - refs)), jnp.pad(row, (0, lanes - slots))])
     vmem = pl.BlockSpec(memory_space=pltpu.VMEM)
     hbm = pl.BlockSpec(memory_space=pl.ANY)
     dma = pltpu.SemaphoreType.DMA
@@ -279,14 +295,15 @@
     count = refs * length
     parts = 4
     query_grad, encoding_grad = pl.pallas_call(
-        functools.partial(kernel, n, spans),
+        functools.partial(kernel, n, spans, length),
         out_shape=(
             jax.ShapeDtypeStruct((toks, width), BF16),
             jax.ShapeDtypeStruct((rows * length, width), BF16),
         ),
-        in_specs=[vmem, vmem, vmem, vmem, hbm, hbm, hbm, hbm],
+        in_specs=[vmem, vmem, hbm, hbm, hbm, hbm],
         out_specs=(hbm, vmem),
         scratch_shapes=[
+            pltpu.VMEM((total, 128), jnp.int32),
             pltpu.VMEM((total, 128), jnp.int32),
             pltpu.VMEM((total, width), BF16),
             pltpu.VMEM((total, width), BF16),
@@ -311,7 +328,7 @@
             collective_id=0, has_side_effects=True, vmem_limit_bytes=58 << 20
         ),
     )(
-        want, place_col, place_row, encodings.reshape(rows * length, width),
+        plan, encodings.reshape(rows * length, width),
         queries, out_grad, key_weight, value_weight,
     )
     return query_grad, encoding_grad.reshape(rows, length, width)

time: 142 us -> 136 us (0.958)
  the two profiles are of different devices: /device:TPU:0 before, /device:TPU:15 now
where the time goes in v3:
time: 136 us
  Pallas kernels  128 us (94%)
  local copies, waits for them, and re-layouts  5.23 us (4%)
  other arithmetic  2.24 us (2%)
    pallas_call x1, Pallas kernels, on_device_whole_heads(): pl.pallas_call(functools.partial(kernel, n, spans, length), out_shape=(ja...  128 us
    unnamed x4, local copies, waits for them, and re-layouts  4.67 us

profile of v3, /device:TPU:15, one launch (start us, length us, event | category | flops | bytes accessed | tf_op | source)
XLA Modules:
  0.0 135.7 jit_solution(13986215455612705284)
XLA Ops:
  0.6 0.7 sign_compare_fusion
  1.3 0.1 copy.14
  1.4 0.1 ne.52
  1.5 0.7 broadcast_divide_fusion
  2.2 0.1 copy.16
  2.3 0.1 div.21
  2.4 0.1 copy.15
  2.5 0.1 rem.33
  2.6 0.2 convert_reduce_fusion
  2.8 0.1 select_reduce_fusion
  2.9 0.6 pad_add_fusion.plan_ref
  3.5 127.5 %shard_map.77 = (bf16[704,2048]{1,0:T(8,128)(2,1)}, bf16[160,2048]{1,0:T(8,128)(2,1)}) custom-call(s32[2,128]{1,0:T(2,128)} %pad_add_fusion.plan_ref, bf16[160,2048]{1,0:T(8,128)(2,1)} %bitcast.6, bf16[704,2048]{1,0:T(8,128)(2,1)} %q_hbm.1, bf16[704,2048]{1,0:T(8,128)(2,1)} %g_hbm.1, bf16[2048,2048]{1,0:T(8,128)(2,1)} %wk_hbm.1, bf16[2048,2048]{1,0:T(8,128)(2,1)} %wv_hbm.1), custom_call_target="tpu_custom_call" | custom-call | tf_op jit(solution)/shard_map/pallas_call | solution.py:297
  131.0 0.0 copy-start
  131.0 3.8 %copy.19 = bf16[704,2048]{1,0:T(8,128)(2,1)} copy(bf16[704,2048]{1,0:T(8,128)(2,1)} %get-tuple-element.14) | data formatting | bytes 5767168
  134.9 0.0 copy-done
  134.9 0.8 copy.20
  (3 shorter events, 0.0 us)
Async XLA Ops:
  131.0 3.8 %copy-start = (bf16[160,2048]{1,0:T(8,128)(2,1)S(1)}, bf16[160,2048]{1,0:T(8,128)(2,1)}, u32[]{:S(2)}) copy-start(bf16[160,2048]{1,0:T(8,128)(2,1)} %get-tuple-element.5) | copy-start | bytes 1966084
